TPU v7x, 256 devices: a whole 4x4x8 slice. The times are simulated.
256 devices in a mesh: tm: 16 (over x_lo, z), expert: 16 (over y, x_hi, core).
Axes of the slice: x: 4 (x_hi: 2, x_lo: 2; x = x_hi * 2 + x_lo), y: 4, z: 8, core: 2. Of those that a mesh axis runs over, the one named last changes fastest.
Arguments:
- frames: float32 [32768, 1536], P(('tm', 'expert')), may hold values from -6 to 6
- lengths: int32 [2], replicated, may hold values from 1 to 24576, 32768 in all
- expert_ids: int32 [32768, 2], P(('tm', 'expert')), may hold values from 0 to 15, all different within a row; in each aligned block of 128 rows (0 to 127, 128 to 255, ...) at most 32 rows name the same one
- w_conv: float32 [31, 1536], replicated, may hold values from -1 to 1
- g_norm: float32 [1536], replicated, may hold values from 0.1 to 1.9
- w_router: float32 [1536, 16], replicated, may hold values from -0.15625 to 0.15625
- w_up: bfloat16 [16, 1536, 1536], P('expert'), may hold values from -0.15625 to 0.15625
- w_down: bfloat16 [16, 1536, 1536], P('expert'), may hold values from -0.15625 to 0.15625
- cotangent: float32 [32768, 1536], P(('tm', 'expert')), may hold values from -6 to 6
Outputs:
- block_out: float32 [32768, 1536], P(('tm', 'expert'))
- frames_grad: float32 [32768, 1536], P(('tm', 'expert'))
- conv_grad: float32 [31, 1536], replicated
- gain_grad: float32 [1536], replicated
- router_grad: float32 [1536, 16], replicated
Inputs may be any that keep to these rules, and one draw needn't show every extreme that they name: `expert_ids`: within the frames of one device (aligned blocks of 128 frames) no expert is named more than 32 times, a bound that some block reaches. The two experts of a frame differ. The lengths sum to 32768; the longest is at most 24576.
All inputs are finite; a program needn't handle non-finite values.
Results may differ from a plain program's by a relative error of at most 0.02.
Values may be sent and summed in bfloat16 or wider, within the bound.
A program may use at most 128 MiB of HBM per device.

v0:
```python
import jax
import jax.numpy as jnp
from jax import lax
from jax.experimental import pallas as pl
from jax.experimental.pallas import tpu as pltpu
from jax.sharding import PartitionSpec as P

EPS = 1e-06
MESH = pl.DeviceIdType.MESH
F32, BF16 = jnp.float32, jnp.bfloat16
EXACT = lax.Precision.HIGHEST

ROWS = 128
D = 1536
TAPS = 31
EDGE = 16
WIDE = ROWS + 2 * EDGE
SPREAD = WIDE + EDGE
MID = ROWS + EDGE
EXPERTS = 16
CAP = 32
SLOTS = EXPERTS * CAP
LANES = 128
BLOCKS = D // LANES
TILE = 256
TILES = D // TILE
GRADS = 48
DE = D + LANES

Y_A, Y_B, Y_C, Y_D = (0, 1), (2, 3), (), ()
EARLY = (0, 1)
NT = (((1,), (1,)), ((), ()))


def sigmoid(v):
    return 0.5 * jnp.tanh(0.5 * v) + 0.5


def spread(wide, bound):
    zeros = jnp.zeros((EDGE, LANES), F32)
    before = jnp.concatenate([wide, zeros], axis=0)
    after = jnp.concatenate([zeros, wide], axis=0)
    row = lax.broadcasted_iota(jnp.int32, (SPREAD, LANES), 0)
    return jnp.where(row < bound, before, jnp.where(row >= bound + EDGE, after, 0.0))


def gather_back(mid, bound):
    row = lax.broadcasted_iota(jnp.int32, (ROWS, LANES), 0) + EDGE
    return jnp.where(row < bound, mid[:ROWS], mid[EDGE:])


def correlate(ref, block, weight_row):
    total = None
    for shift in range(8):
        rows = ref[block, shift : shift + MID + 24, :]
        for whole in range(4):
            tap = 8 * whole + shift - 1
            if 0 <= tap < TAPS:
                term = weight_row(tap) * rows[8 * whole : 8 * whole + MID]
                total = term if total is None else total + term
    return total


def body(
    len_hbm, ids_hbm, wconv_hbm, gain_hbm, wr_hbm, frames_hbm, cot_hbm, wup_hbm, wdn_hbm,
    outv, dfrv, convv, gainv, routerv,
    len_ref, ids_ref, wconv_ref, gain_ref, wr_ref, wrb,
    fr, cot, wup, wdn, gw, gd, pre, mixed, dmix,
    normed, cotb,
    onehot, pick, send_c, recv_c, send_x, recv_x, ret_y, got_y, ret_d, got_d,
    dhid, hid, dup, py, pd, pg, parts,
    halo_s, halo_r, ar_src, ar_in, mid_src, mid_in, fin_src, fin,
    lsem, ssem, rsem, hs, hr, a1s, a1r, a2s, a2r, a3s, a3r, known,
):
    tm, ex = lax.axis_index("tm"), lax.axis_index("expert")
    xl, z = tm // 8, tm % 8
    y, xh, core = ex // 4, (ex // 2) % 2, ex % 2
    lin = tm * EXPERTS + ex

    def peer(r):
        b, dy = r // 4, r % 4
        fx, dc = (dy + b // 2) % 2, b % 2
        return {
            "tm": ((xl + fx) % 2) * 8 + z,
            "expert": ((y + dy) % 4) * 4 + ((xh + fx) % 2) * 2 + (core + dc) % 2,
        }

    def back(r):
        return (r // 4) * 4 + (4 - r % 4) % 4

    def of_expert(e):
        dy, fx, dc = (e // 4 + 4 - y) % 4, (e // 2 + xh) % 2, (e + core) % 2
        return 4 * (2 * ((dy + fx) % 2) + dc) + dy

    def column(k):
        return {"tm": (tm + k) % 16, "expert": ex}

    def along(step):
        return {"tm": xl * 8 + (z + 8 + step) % 8, "expert": ex}

    def beside(step):
        other = (lin + 256 + step) % 256
        return {"tm": other // EXPERTS, "expert": other % EXPERTS}

    barrier = pltpu.get_barrier_semaphore()
    hails = [peer(r) for r in (6, 2, 14, 10, 7, 5, 3, 1, 15, 13, 11, 9, 12, 8, 4)]
    hails = hails[:4] + [beside(1), beside(-1)] + hails[4:] + [along(1), along(-1), column(8)]
    loads = [
        pltpu.make_async_copy(frames_hbm, fr, lsem.at[0]),
        pltpu.make_async_copy(cot_hbm, cot, lsem.at[1]),
        pltpu.make_async_copy(wdn_hbm.at[0], wdn, lsem.at[2]),
        pltpu.make_async_copy(wup_hbm.at[0], wup, lsem.at[3]),
        pltpu.make_async_copy(ids_hbm, ids_ref, lsem.at[4]),
        pltpu.make_async_copy(wconv_hbm, wconv_ref, lsem.at[5]),
        pltpu.make_async_copy(gain_hbm, gain_ref, lsem.at[6]),
        pltpu.make_async_copy(wr_hbm, wr_ref, lsem.at[7]),
        pltpu.make_async_copy(len_hbm, len_ref, lsem.at[8]),
    ]
    for n in (4, 0, 1):
        loads[n].start()
    for other in hails:
        pl.semaphore_signal(barrier, inc=1, device_id=other, device_id_type=MESH)
    for n in (8, 5, 6, 7, 2, 3):
        loads[n].start()

    loads[4].wait()
    def upright(row):
        return jnp.broadcast_to(row.astype(F32), (LANES, ROWS)).T.astype(jnp.int32)

    ids0, ids1 = upright(ids_ref[0:1, :]), upright(ids_ref[1:2, :])

    def relative(e):
        dy, fx, dc = ((e >> 2) - y) & 3, ((e >> 1) & 1) ^ xh, (e & 1) ^ core
        return (((dy ^ fx) & 1) << 3) | (dc << 2) | dy

    rel0, rel1 = relative(ids0), relative(ids1)
    lane = lax.broadcasted_iota(jnp.int32, (ROWS, LANES), 1)
    sub = lax.broadcasted_iota(jnp.int32, (ROWS, LANES), 0)
    names0 = jnp.where(rel0 == lane, 1.0, 0.0).astype(F32)
    names1 = jnp.where(rel1 == lane, 1.0, 0.0).astype(F32)
    names = names0 + names1
    earlier = jnp.where(lane < sub, 1.0, 0.0).astype(F32)
    later = jnp.where(sub < lane, 1.0, 0.0).astype(F32)
    rank = jnp.dot(earlier.astype(BF16), names.astype(BF16), preferred_element_type=F32)
    rank0 = jnp.sum(names0 * rank, axis=1, keepdims=True).astype(jnp.int32)
    rank1 = jnp.sum(names1 * rank, axis=1, keepdims=True).astype(jnp.int32)
    slot0, slot1 = rel0 * CAP + rank0, rel1 * CAP + rank1
    for b in range(4):
        here = slice(b * LANES, (b + 1) * LANES)
        pick[0:ROWS, here] = jnp.where(lane + b * LANES == slot0, 1.0, 0.0).astype(BF16)
        pick[ROWS : 2 * ROWS, here] = jnp.where(lane + b * LANES == slot1, 1.0, 0.0).astype(BF16)
    by_expert = names.T
    order = jnp.dot(by_expert.astype(BF16), later.astype(BF16), preferred_element_type=F32)
    order = jnp.where(by_expert > 0.5, order, -1.0)
    place = lax.broadcasted_iota(jnp.int32, (CAP, LANES), 0).astype(F32)
    for r in range(EXPERTS):
        onehot[r * CAP : (r + 1) * CAP, :] = jnp.where(
            order[r : r + 1, :] == place, 1.0, 0.0
        ).astype(BF16)

    loads[0].wait()
    halo_s[0] = fr[0:EDGE, :].astype(BF16)
    halo_s[1] = fr[ROWS - EDGE : ROWS, :].astype(BF16)

    def halo(stage, side):
        n = 2 * stage + side
        return pltpu.make_async_remote_copy(
            src_ref=halo_s.at[n],
            dst_ref=halo_r.at[2 * stage + 1 - side],
            send_sem=hs.at[n],
            recv_sem=hr.at[2 * stage + 1 - side],
            device_id=beside(2 * side - 1),
            device_id_type=MESH,
        )

    def rows_of(ref, r):
        return ref.at[pl.ds(pl.multiple_of(r * CAP, CAP), CAP), :]

    def trade(kind, src, dst, r):
        return pltpu.make_async_remote_copy(
            src_ref=rows_of(src, r),
            dst_ref=rows_of(dst, back(r)),
            send_sem=ssem.at[kind, r],
            recv_sem=rsem.at[kind, back(r)],
            device_id=peer(r),
            device_id_type=MESH,
        )

    def start_batch(kind, src, dst, b):
        def one(i, carry):
            r = 4 * b + i

            @pl.when(r != 0)
            def _():
                trade(kind, src, dst, r).start()

            return carry

        lax.fori_loop(0, 4, one, 0)

    def arrive_batch(kind, src, dst, b):
        def one(i, carry):
            r = 4 * b + i

            @pl.when(r != 0)
            def _():
                trade(kind, src, dst, back(r)).wait_recv()

            return carry

        lax.fori_loop(0, 4, one, 0)

    def cols(n, width=TILE):
        return pl.ds(pl.multiple_of(n * width, width), width)

    def batch(b):
        return pl.ds(pl.multiple_of(b * ROWS, ROWS), ROWS)

    def fill(source, src, b):
        def part(n, inner):
            src[batch(b), cols(n)] = jnp.dot(
                onehot[batch(b), :], source[:, cols(n)], preferred_element_type=F32
            ).astype(BF16)
            return inner

        lax.fori_loop(0, TILES, part, 0)

    loads[1].wait()

    def narrow(n, carry):
        cotb[:, cols(n)] = cot[:, cols(n)].astype(BF16)
        return carry

    lax.fori_loop(0, TILES, narrow, 0)

    def fill_c(b, carry):
        fill(cotb, send_c, b)
        return carry

    lax.fori_loop(0, 4, fill_c, 0)
    pl.semaphore_wait(barrier, len(hails))
    halo(0, 0).start()
    halo(0, 1).start()

    def go_c(b, carry):
        start_batch(0, send_c, recv_c, b)
        return carry

    lax.fori_loop(0, 4, go_c, 0)
    recv_c[0:CAP, :] = send_c[0:CAP, :]

    def tell(n):
        pl.semaphore_signal(known.at[2 * n], inc=1, device_id=along(1), device_id_type=MESH)
        pl.semaphore_signal(known.at[2 * n + 1], inc=1, device_id=along(-1), device_id_type=MESH)

    def hear(n):
        pl.semaphore_wait(known.at[2 * n], 1)
        pl.semaphore_wait(known.at[2 * n + 1], 1)

    tell(0)

    loads[8].wait()
    loads[5].wait()
    bound = len_ref[0] - lin * ROWS + EDGE
    bound = jnp.where((bound >= 1) & (bound < WIDE), bound, 4 * SPREAD)
    halo(0, 1).wait_recv()
    halo(0, 0).wait_recv()

    def widen(n, middle, stage, m):
        low = jnp.where(lin == 0, 0.0, halo_r[2 * stage, :, cols(m, LANES)].astype(F32))
        high = jnp.where(lin == 255, 0.0, halo_r[2 * stage + 1, :, cols(m, LANES)].astype(F32))
        return jnp.concatenate([low, middle, high], axis=0)

    def conv(m, squares):
        here = cols(m, LANES)
        gw[m] = spread(widen(0, fr[:, here], 0, m), bound)
        total = correlate(gw, m, lambda tap: wconv_ref[tap : tap + 1, here])
        act = gather_back(total, bound)
        row = fr[:, here] + act * sigmoid(act)
        pre[:, here] = act
        mixed[:, here] = row
        return squares + row * row

    squares = lax.fori_loop(0, BLOCKS, conv, jnp.zeros((ROWS, LANES), F32))
    inv = lax.rsqrt(jnp.sum(squares, axis=1, keepdims=True) * (1.0 / D) + EPS)

    loads[6].wait()

    def gain(here):
        return gain_ref[here].reshape(1, LANES)

    def norm(m, carry):
        here = cols(m, LANES)
        normed[:, here] = (mixed[:, here] * inv * gain(here)).astype(BF16)
        return carry

    lax.fori_loop(0, BLOCKS, norm, 0)

    def go_x(b, carry):
        fill(normed, send_x, b)
        start_batch(1, send_x, recv_x, b)
        return carry

    lax.fori_loop(0, 4, go_x, 0)
    recv_x[0:CAP, :] = send_x[0:CAP, :]
    hear(0)
    tell(1)

    loads[7].wait()
    router_f = wr_ref[...]
    part0 = router_f.astype(BF16)
    rest = router_f - part0.astype(F32)
    part1 = rest.astype(BF16)
    wrb[0:16, :] = part0
    wrb[16:32, :] = part1
    wrb[32:48, :] = (rest - part1.astype(F32)).astype(BF16)
    wrb[48:64, :] = part0
    wrb[64:128, :] = jnp.zeros((64, D), BF16)
    logits = lax.dot_general(normed[...], wrb[...], NT, preferred_element_type=F32)
    logits = jnp.where(lane < 48, logits, 0.0)
    low = lane & 15
    top0 = jnp.sum(jnp.where(ids0 == low, logits, 0.0), axis=1, keepdims=True)
    top1 = jnp.sum(jnp.where(ids1 == low, logits, 0.0), axis=1, keepdims=True)
    most = jnp.maximum(top0, top1)
    exp0, exp1 = jnp.exp(top0 - most), jnp.exp(top1 - most)
    gate0, gate1 = exp0 / (exp0 + exp1), exp1 / (exp0 + exp1)

    loads[2].wait()

    def hidden_grad(b, carry):
        arrive_batch(0, send_c, recv_c, b)

        def part(n, inner):
            dhid[batch(b), cols(n)] = lax.dot_general(
                recv_c[batch(b), :], wdn[cols(n), :], NT, preferred_element_type=F32
            ).astype(BF16)
            return inner

        lax.fori_loop(0, TILES, part, 0)
        return carry

    lax.fori_loop(0, 4, hidden_grad, 0)
    hear(1)
    tell(2)
    loads[3].wait()

    def expert(b, carry):
        arrive_batch(1, send_x, recv_x, b)

        def up(n, dots):
            u = jnp.dot(recv_x[batch(b), :], wup[:, cols(n)], preferred_element_type=F32)
            s = sigmoid(u)
            h = (u * s).astype(BF16)
            hid[batch(b), cols(n)] = h
            slope = s * (1.0 + u * (1.0 - s))
            dh = dhid[batch(b), cols(n)].astype(F32)
            dup[:, cols(n)] = (dh * slope).astype(BF16)
            dot = dh * h.astype(F32)
            return dots + dot[:, :LANES] + dot[:, LANES:]

        def rows_grad(n, inner):
            ret_d[batch(b), cols(n)] = lax.dot_general(
                dup[...], wup[cols(n), :], NT, preferred_element_type=F32
            ).astype(BF16)
            return inner

        dots = lax.fori_loop(0, TILES, up, jnp.zeros((ROWS, LANES), F32))
        dgate = jnp.sum(dots, axis=1, keepdims=True)
        first = dgate.astype(BF16).astype(F32)
        ret_d[batch(b), D:DE] = jnp.where(
            lane == 0, first, jnp.where(lane == 1, dgate - first, 0.0)
        ).astype(BF16)
        lax.fori_loop(0, TILES, rows_grad, 0)
        start_batch(3, ret_d, got_d, b)
        return carry

    lax.fori_loop(0, 4, expert, 0)
    got_d[0:CAP, :] = ret_d[0:CAP, :]

    def down(b, carry):
        def part(n, inner):
            ret_y[batch(b), cols(n)] = jnp.dot(
                hid[batch(b), :], wdn[:, cols(n)], preferred_element_type=F32
            ).astype(BF16)
            return inner

        lax.fori_loop(0, TILES, part, 0)
        return carry

    lax.fori_loop(0, 4, down, 0)
    got_y[0:CAP, :] = ret_y[0:CAP, :]

    def go_y(batches):
        for b in batches:
            start_batch(2, ret_y, got_y, b)

    go_y(Y_A)
    hear(2)
    tell(3)

    def collect(kind, src, got, total, tail, batches):
        for b in batches:
            arrive_batch(kind, src, got, b)
            chosen = pick[:, b * ROWS : (b + 1) * ROWS]

            def part(n, carry):
                term = jnp.dot(chosen, got[batch(b), cols(n)], preferred_element_type=F32)
                total[:, cols(n)] = term if b == 0 else total[:, cols(n)] + term
                return carry

            lax.fori_loop(0, TILES, part, 0)
            if tail is not None:
                term = jnp.dot(chosen, got[batch(b), D:DE], preferred_element_type=F32)
                tail[...] = term if b == 0 else tail[...] + term

    collect(3, ret_d, got_d, pd, pg, range(4))
    dgates = jnp.sum(pg[...], axis=1, keepdims=True)
    dtop = gate0 * gate1 * (dgates[0:ROWS] - dgates[ROWS : 2 * ROWS])
    first = dtop.astype(BF16).astype(F32)
    second = dtop - first
    amount = jnp.where(lane < 48, first, jnp.where(lane < 64, second, 0.0))
    dlogits = jnp.where(ids0 == low, amount, 0.0) - jnp.where(ids1 == low, amount, 0.0)
    dlogits_t = dlogits.T[32:64, :].astype(BF16)
    dlogits = dlogits.astype(BF16)

    def router(n, carry):
        both = jnp.dot(dlogits_t, normed[:, cols(n)], preferred_element_type=F32)
        both = (both[0:16] + both[16:32]).astype(BF16)
        ar_src[2 * n, 32:48, :] = both[:, :LANES]
        ar_src[2 * n + 1, 32:48, :] = both[:, LANES:]
        dmix[:, cols(n)] = jnp.dot(dlogits, wrb[:, cols(n)], preferred_element_type=F32)
        return carry

    lax.fori_loop(0, TILES, router, 0)

    def norm_back(m, sums):
        here = cols(m, LANES)
        dn = gate0 * pd[0:ROWS, here] + gate1 * pd[ROWS : 2 * ROWS, here] + dmix[:, here]
        row = mixed[:, here]
        parts[m, 0:8, :] = jnp.sum((dn * row * inv).reshape(ROWS // 8, 8, LANES), axis=0)
        dn = dn * gain(here)
        pd[0:ROWS, here] = dn
        return sums + dn * row

    sums = lax.fori_loop(0, BLOCKS, norm_back, jnp.zeros((ROWS, LANES), F32))
    pull = inv * inv * inv * (jnp.sum(sums, axis=1, keepdims=True) * (1.0 / D))

    def act_back(m, carry):
        here = cols(m, LANES)
        dm = cot[:, here] + (inv * pd[0:ROWS, here] - mixed[:, here] * pull)
        act = pre[:, here]
        s = sigmoid(act)
        dp = dm * (s * (1.0 + act * (1.0 - s)))
        dmix[:, here] = dm
        pd[ROWS : 2 * ROWS, here] = dp
        halo_s[2, :, here] = dp[0:EDGE].astype(BF16)
        halo_s[3, :, here] = dp[ROWS - EDGE : ROWS].astype(BF16)
        return carry

    lax.fori_loop(0, BLOCKS, act_back, 0)
    halo(1, 0).start()
    halo(1, 1).start()

    rows32 = lax.broadcasted_iota(jnp.int32, (32, 512), 0)
    lanes32 = lax.broadcasted_iota(jnp.int32, (32, 512), 1)
    fold = jnp.where(((lanes32 & 255) >> 3) == rows32, 1.0, 0.0).astype(BF16)

    def to_owner(m):
        r = of_expert(m)
        return pltpu.make_async_remote_copy(
            src_ref=ar_src.at[m],
            dst_ref=ar_in.at[back(r)],
            send_sem=a1s.at[m],
            recv_sem=a1r.at[back(r)],
            device_id=peer(r),
            device_id_type=MESH,
        )

    def kernel_grad(i, carry):
        m = (i + ex) % BLOCKS
        here = cols(m, LANES)
        edge = jnp.zeros((EDGE, LANES), F32)
        mid = spread(jnp.concatenate([edge, pd[ROWS : 2 * ROWS, here], edge], axis=0), bound)
        mid = mid[EDGE : EDGE + MID]
        terms = [None] * TAPS
        for shift in range(8):
            rows = gw[m, shift : shift + MID + 24, :]
            for whole in range(4):
                tap = 8 * whole + shift - 1
                if 0 <= tap < TAPS:
                    product = mid * rows[8 * whole : 8 * whole + MID]
                    terms[tap] = jnp.sum(product.reshape(MID // 8, 8, LANES), axis=0)
        terms.append(parts[m, 0:8, :])
        terms = jnp.concatenate(terms, axis=0)
        first = terms.astype(BF16)
        second = (terms - first.astype(F32)).astype(BF16)
        ar_src[m, 0:32, :] = jnp.dot(
            fold, jnp.concatenate([first, second], axis=0), preferred_element_type=F32
        ).astype(BF16)

        @pl.when(m != ex)
        def _():
            to_owner(m).start()

        return carry

    lax.fori_loop(0, BLOCKS, kernel_grad, 0)
    go_y(Y_B)
    hear(3)

    halo(1, 1).wait_recv()
    halo(1, 0).wait_recv()

    def frames_back(m, carry):
        here = cols(m, LANES)
        gd[0] = spread(widen(0, pd[ROWS : 2 * ROWS, here], 1, m), bound)
        total = correlate(gd, 0, lambda tap: wconv_ref[TAPS - 1 - tap : TAPS - tap, here])
        dfrv[:, here] = dmix[:, here] + gather_back(total, bound)
        return carry

    lax.fori_loop(0, BLOCKS, frames_back, 0)

    def over_columns(k):
        return pltpu.make_async_remote_copy(
            src_ref=mid_src,
            dst_ref=mid_in.at[16 - k],
            send_sem=a2s.at[k],
            recv_sem=a2r.at[16 - k],
            device_id=column(k),
            device_id_type=MESH,
        )

    def to_all(r):
        return pltpu.make_async_remote_copy(
            src_ref=fin_src,
            dst_ref=fin.at[ex],
            send_sem=a3s.at[r],
            recv_sem=a3r.at[ex],
            device_id=peer(r),
            device_id_type=MESH,
        )

    @pl.when(ex < BLOCKS)
    def _():
        def add(q, total):
            pltpu.make_async_remote_copy(
                src_ref=ar_src.at[0],
                dst_ref=ar_in.at[q],
                send_sem=a1s.at[0],
                recv_sem=a1r.at[q],
                device_id=peer(q),
                device_id_type=MESH,
            ).wait_recv()
            return total + ar_in[q].astype(F32)

        total = lax.fori_loop(1, 16, add, ar_src[ex].astype(F32))
        mid_src[...] = total.astype(BF16)

        def send(k, carry):
            over_columns(k).start()
            return carry

        lax.fori_loop(1, 16, send, 0)

    go_y(Y_C)
    collect(2, ret_y, got_y, py, None, EARLY)

    @pl.when(ex < BLOCKS)
    def _():
        def add(k, total):
            over_columns(16 - k).wait_recv()
            return total + mid_in[k].astype(F32)

        total = lax.fori_loop(1, 16, add, mid_src[...].astype(F32))
        fin_src[...] = total.astype(BF16)

        def send(r, carry):
            to_all(r).start()
            return carry

        lax.fori_loop(1, 16, send, 0)
        fin[ex] = fin_src[...]

    go_y(Y_D)
    collect(2, ret_y, got_y, py, None, range(len(EARLY), 4))

    def finish(m, carry):
        here = cols(m, LANES)
        outv[:, here] = mixed[:, here] + (
            gate0 * py[0:ROWS, here] + gate1 * py[ROWS : 2 * ROWS, here]
        )
        return carry

    lax.fori_loop(0, BLOCKS, finish, 0)

    def spread_out(m, carry):
        @pl.when(m != ex)
        def _():
            pltpu.make_async_remote_copy(
                src_ref=fin_src,
                dst_ref=fin.at[m],
                send_sem=a3s.at[0],
                recv_sem=a3r.at[m],
                device_id=peer(of_expert(m)),
                device_id_type=MESH,
            ).wait_recv()

        here = cols(m, LANES)
        block = fin[m].astype(F32)
        convv[:, here] = block[0:TAPS]
        gainv[here] = block[TAPS]
        routerv[:, here] = block[32:48]
        return carry

    lax.fori_loop(0, BLOCKS, spread_out, 0)

    def sent(r, carry):
        trade(0, send_c, recv_c, r).wait_send()
        trade(1, send_x, recv_x, r).wait_send()
        trade(2, ret_y, got_y, r).wait_send()
        trade(3, ret_d, got_d, r).wait_send()
        return carry

    lax.fori_loop(1, 16, sent, 0)

    def sent_owner(m, carry):
        @pl.when(m != ex)
        def _():
            to_owner(m).wait_send()

        return carry

    lax.fori_loop(0, BLOCKS, sent_owner, 0)

    @pl.when(ex < BLOCKS)
    def _():
        def done(k, carry):
            over_columns(k).wait_send()
            to_all(k).wait_send()
            return carry

        lax.fori_loop(1, 16, done, 0)

    for stage in range(2):
        for side in range(2):
            halo(stage, side).wait_send()


def hand_over(*refs):
    count = (len(refs) - 1) // 2
    copies = [
        pltpu.make_async_copy(refs[n], refs[count + n], refs[-1].at[n]) for n in range(count)
    ]
    for copy in copies:
        copy.start()
    for copy in copies:
        copy.wait()


def on_device(frames, lengths, expert_ids, w_conv, g_norm, w_router, w_up, w_down, cotangent):
    anywhere = pl.BlockSpec(memory_space=pl.ANY)
    wide_f = pltpu.VMEM((ROWS, D), F32)
    half = pltpu.VMEM((ROWS, D), BF16)
    slots = pltpu.VMEM((SLOTS, D), BF16)
    returned = pltpu.VMEM((SLOTS, DE), BF16)
    weight = pltpu.VMEM((D, D), BF16)
    dma = pltpu.SemaphoreType.DMA
    results = (
        jax.ShapeDtypeStruct((ROWS, D), F32),
        jax.ShapeDtypeStruct((ROWS, D), F32),
        jax.ShapeDtypeStruct((TAPS, D), F32),
        jax.ShapeDtypeStruct((D,), F32),
        jax.ShapeDtypeStruct((EXPERTS, D), F32),
    )
    vmem = pl.BlockSpec(memory_space=pltpu.VMEM)
    held = pl.pallas_call(
        body,
        out_shape=tuple(pltpu.VMEM(r.shape, r.dtype) for r in results),
        in_specs=[anywhere] * 9,
        out_specs=(vmem,) * 5,
        scratch_shapes=[
            pltpu.SMEM((2,), jnp.int32), pltpu.VMEM((2, ROWS), jnp.int32),
            pltpu.VMEM((TAPS, D), F32), pltpu.VMEM((D,), F32), pltpu.VMEM((EXPERTS, D), F32),
            half,
            wide_f, wide_f, weight, weight,
            pltpu.VMEM((BLOCKS, SPREAD, LANES), F32),
            pltpu.VMEM((1, SPREAD, LANES), F32),
            wide_f, wide_f, wide_f,
            half, half,
            pltpu.VMEM((SLOTS, ROWS), BF16), pltpu.VMEM((2 * ROWS, SLOTS), BF16),
            slots, slots, slots, slots, slots, slots, returned, returned,
            slots, slots, half,
            pltpu.VMEM((2 * ROWS, D), F32), pltpu.VMEM((2 * ROWS, D), F32),
            pltpu.VMEM((2 * ROWS, LANES), F32),
            pltpu.VMEM((BLOCKS, 8, LANES), F32),
            pltpu.VMEM((4, EDGE, D), BF16), pltpu.VMEM((4, EDGE, D), BF16),
            pltpu.VMEM((BLOCKS, GRADS, LANES), BF16), pltpu.VMEM((16, GRADS, LANES), BF16),
            pltpu.VMEM((GRADS, LANES), BF16), pltpu.VMEM((16, GRADS, LANES), BF16),
            pltpu.VMEM((GRADS, LANES), BF16), pltpu.VMEM((BLOCKS, GRADS, LANES), BF16),
            dma((9,)), dma((4, 16)), dma((4, 16)), dma((4,)), dma((4,)),
            dma((BLOCKS,)), dma((16,)), dma((16,)), dma((16,)), dma((16,)), dma((BLOCKS,)),
            pltpu.SemaphoreType.REGULAR((8,)),
        ],
        compiler_params=pltpu.CompilerParams(
            collective_id=0, has_side_effects=True, vmem_limit_bytes=56 * 2**20
        ),
    )(
        lengths, expert_ids.T, w_conv, g_norm, w_router.T, frames, cotangent, w_up, w_down
    )
    block_out, frames_grad, conv, gain, router = pl.pallas_call(
        hand_over,
        out_shape=results,
        in_specs=[vmem] * 5,
        out_specs=(anywhere,) * 5,
        scratch_shapes=[dma((5,))],
        compiler_params=pltpu.CompilerParams(vmem_limit_bytes=2**20),
    )(*held)
    return block_out, frames_grad, conv, gain, router.T


def solution(mesh):
    placed = (
        P(("tm", "expert"), None),
        P(),
        P(("tm", "expert"), None),
        P(),
        P(),
        P(),
        P("expert", None, None),
        P("expert", None, None),
        P(("tm", "expert"), None),
    )
    return jax.shard_map(
        on_device,
        mesh=mesh,
        in_specs=placed,
        out_specs=(P(("tm", "expert"), None), P(("tm", "expert"), None), P(), P(), P()),
        check_vma=False,
    )
```

profile of v0, /device:TPU:1, one launch (start us, length us, event | category | flops | bytes accessed | tf_op | source)
XLA Modules:
  0.0 100.3 jit_solution(16416135463511414627)
XLA Ops:
  0.6 98.4 %shard_map.128 = (f32[128,1536]{1,0:T(8,128)S(1)}, f32[128,1536]{1,0:T(8,128)S(1)}, f32[31,1536]{1,0:T(8,128)S(1)}, f32[1536]{0:T(1024)S(1)}, f32[16,1536]{1,0:T(8,128)S(1)}) custom-call(s32[2]{0:T(128)} %len_hbm.1, s32[2,128]{1,0:T(2,128)} %bitcast.4, f32[31,1536]{1,0:T(8,128)} %wconv_hbm.1, f32[1536]{0:T(1024)} %gain_hbm.1, f32[16,1536]{1,0:T(8,128)} %bitcast.3, ...), custom_call_target="tpu_custom_call" | custom-call | tf_op jit(solution)/shard_map/pallas_call | solution.py:676
  99.0 1.3 %shard_map.129 = (f32[128,1536]{1,0:T(8,128)}, f32[128,1536]{1,0:T(8,128)}, f32[31,1536]{1,0:T(8,128)}, f32[1536]{0:T(1024)}, f32[16,1536]{1,0:T(8,128)}) custom-call(f32[128,1536]{1,0:T(8,128)S(1)} %get-tuple-element.15.refs_0_, f32[128,1536]{1,0:T(8,128)S(1)} %get-tuple-element.16.refs_1_, f32[31,1536]{1,0:T(8,128)S(1)} %get-tuple-element.17.refs_2_, ...), custom_call_target="tpu_custom_call" | custom-call | tf_op jit(solution)/shard_map/pallas_call | solution.py:710
where the time goes:
time: 100 us
  Pallas kernels  99.6 us (100%)
    pallas_call x1, Pallas kernels, on_device(): pl.pallas_call(body, out_shape=tuple((pltpu.VMEM(r.shape, r.dtype) for r...  98.4 us

commit v1 on v0

--- a/solution.py
+++ b/solution.py
@@ -120,7 +120,7 @@
         loads[n].start()
     for other in hails:
         pl.semaphore_signal(barrier, inc=1, device_id=other, device_id_type=MESH)
-    for n in (8, 5, 6, 7, 2, 3):
+    for n in (8, 5, 6, 7):
         loads[n].start()
 
     loads[4].wait()
@@ -239,14 +239,17 @@
 
     lax.fori_loop(0, 4, fill_c, 0)
     pl.semaphore_wait(barrier, len(hails))
+
+    def go_c(b, carry):
+        start_batch(0, send_c, recv_c, b)
+        return carry
+
+    for r in range(1, 16):
+        trade(0, send_c, recv_c, r).start()
+    for n in (2, 3):
+        loads[n].start()
     halo(0, 0).start()
     halo(0, 1).start()
-
-    def go_c(b, carry):
-        start_batch(0, send_c, recv_c, b)
-        return carry
-
-    lax.fori_loop(0, 4, go_c, 0)
     recv_c[0:CAP, :] = send_c[0:CAP, :]
 
     def tell(n):
@@ -556,11 +559,8 @@
         total = lax.fori_loop(1, 16, add, ar_src[ex].astype(F32))
         mid_src[...] = total.astype(BF16)
 
-        def send(k, carry):
+        for k in (4, 12, 3, 11, 5, 13, 2, 10, 6, 14, 1, 7, 9, 15, 8):
             over_columns(k).start()
-            return carry
-
-        lax.fori_loop(1, 16, send, 0)
 
     go_y(Y_C)
     collect(2, ret_y, got_y, py, None, EARLY)
@@ -574,11 +574,8 @@
         total = lax.fori_loop(1, 16, add, mid_src[...].astype(F32))
         fin_src[...] = total.astype(BF16)
 
-        def send(r, carry):
+        for r in (6, 2, 14, 10, 7, 5, 3, 1, 15, 13, 11, 9, 12, 8, 4):
             to_all(r).start()
-            return carry
-
-        lax.fori_loop(1, 16, send, 0)
         fin[ex] = fin_src[...]
 
     go_y(Y_D)

time: 100 us -> 99 us (0.990)
  Pallas kernels: 99.6 us -> 98.2 us
    pallas_call x1, Pallas kernels: 98.4 us -> 96.9 us  [on_device(): pl.pallas_call(body, out_shape=tuple((pltpu.VMEM(r.shape, r.dtype) for r...]
where the time goes in v1:
time: 99 us; the launch traced here: 98.8 us
  Pallas kernels  98.2 us (99%)
    pallas_call x1, Pallas kernels, on_device(): pl.pallas_call(body, out_shape=tuple((pltpu.VMEM(r.shape, r.dtype) for r...  96.9 us

profile of v1, /device:TPU:1, one launch (start us, length us, event | category | flops | bytes accessed | tf_op | source)
XLA Modules:
  0.0 98.8 jit_solution(10755906736191783758)
XLA Ops:
  0.6 96.9 %shard_map.128 = (f32[128,1536]{1,0:T(8,128)S(1)}, f32[128,1536]{1,0:T(8,128)S(1)}, f32[31,1536]{1,0:T(8,128)S(1)}, f32[1536]{0:T(1024)S(1)}, f32[16,1536]{1,0:T(8,128)S(1)}) custom-call(s32[2]{0:T(128)} %len_hbm.1, s32[2,128]{1,0:T(2,128)} %bitcast.4, f32[31,1536]{1,0:T(8,128)} %wconv_hbm.1, f32[1536]{0:T(1024)} %gain_hbm.1, f32[16,1536]{1,0:T(8,128)} %bitcast.3, ...), custom_call_target="tpu_custom_call" | custom-call | tf_op jit(solution)/shard_map/pallas_call | solution.py:673
  97.6 1.3 %shard_map.129 = (f32[128,1536]{1,0:T(8,128)}, f32[128,1536]{1,0:T(8,128)}, f32[31,1536]{1,0:T(8,128)}, f32[1536]{0:T(1024)}, f32[16,1536]{1,0:T(8,128)}) custom-call(f32[128,1536]{1,0:T(8,128)S(1)} %get-tuple-element.15.refs_0_, f32[128,1536]{1,0:T(8,128)S(1)} %get-tuple-element.16.refs_1_, f32[31,1536]{1,0:T(8,128)S(1)} %get-tuple-element.17.refs_2_, ...), custom_call_target="tpu_custom_call" | custom-call | tf_op jit(solution)/shard_map/pallas_call | solution.py:707
